TPU v7x, 32 devices: a whole 2x2x4 slice. The times are simulated.
32 devices in a mesh: rep: 2 (over x), grp: 8 (over z, y), loc: 2 (over core).
Axes of the slice: x: 2, y: 2, z: 4, core: 2. Of those that a mesh axis runs over, the one named last changes fastest.
Arguments:
- tokens: bfloat16 [4096, 3584], P(('rep', 'grp', 'loc')), parts along dimension 0, may hold values from -6 to 6
- route_groups: int32 [4096, 4], P(('rep', 'grp', 'loc')), parts along dimension 0, may hold values from 0 to 7, as said below
- route_weights: int32 [4096, 8], P(('rep', 'grp', 'loc')), parts along dimension 0, may hold values from 256 to 2040, as said below
- gate_weight: bfloat16 [16, 3584, 1024], P(('grp', 'loc')), may hold values from -0.09375 to 0.09375
- up_weight: bfloat16 [16, 3584, 1024], P(('grp', 'loc')), may hold values from -0.09375 to 0.09375
- down_weight: bfloat16 [16, 1024, 3584], P(('grp', 'loc')), may hold values from -0.1875 to 0.1875
Outputs:
- mixed: bfloat16 [4096, 3584], P(('rep', 'grp', 'loc')), parts along dimension 0
There are 2 independent parts, one for each index of `rep`. A program takes and returns all parts, laid end to end along the dimension named above; an argument that names none is the same for every part. Nothing has to cross between parts.
Inputs may be any that keep to these rules, and one draw needn't show every extreme that they name: `route_groups`: each token names 4 distinct groups. Among the 128 tokens of one device no group is named by more than 80 tokens, and one group, the same on every device of a replica, is named by exactly 80 of them. `route_weights`: multiples of 8.
All inputs are finite; a program needn't handle non-finite values.
Results may differ from a plain program's by a relative error of at most 0.0065.
Values may be sent and summed in bfloat16 or wider, within the bound.
A program may use at most 128 MiB of HBM per device.

v0:
```python
import jax
import jax.numpy as jnp
from jax import lax
from jax.sharding import PartitionSpec as P


def shards(tokens, route_groups, route_weights, gate_weight, up_weight, down_weight):
    n_rows, width = tokens.shape
    n_group = lax.axis_size("grp")
    n_loc = lax.axis_size("loc")
    top_groups = route_groups.shape[1]
    capacity = n_rows * top_groups * 5 // (n_group * 4)
    n_src = n_group * n_loc
    axes = ("grp", "loc")

    routing = jnp.concatenate([route_groups, route_weights], axis=1)
    routing = lax.all_gather(routing, axes, axis=0, tiled=False)
    everyone = lax.all_gather(tokens, axes, axis=0, tiled=False)

    group = lax.axis_index("grp")
    local = lax.axis_index("loc")
    hit = routing[:, :, :top_groups] == group
    weights = routing[:, :, top_groups:].reshape(n_src, n_rows, top_groups, n_loc)
    mine = jnp.sum(
        jnp.where(jnp.arange(n_loc, dtype=jnp.int32) == local, weights, 0), axis=3
    )
    share = jnp.sum(jnp.where(hit, mine, 0), axis=2).astype(jnp.float32) / 4096.0
    picked = jnp.any(hit, axis=2).astype(jnp.int32)
    slots = jnp.cumsum(picked, axis=1) - picked
    assign = (picked[:, None, :] == 1) & (
        slots[:, None, :] == jnp.arange(capacity, dtype=jnp.int32)[None, :, None]
    )
    slot_share = jnp.sum(jnp.where(assign, share[:, None, :], 0.0), axis=2)
    place = assign.astype(jnp.bfloat16)
    rows = jnp.einsum(
        "sqt,std->sqd", place, everyone, preferred_element_type=jnp.float32
    ).astype(jnp.bfloat16).reshape(n_src * capacity, width)
    gate = jnp.dot(rows, gate_weight[0], preferred_element_type=jnp.float32)
    upper = jnp.dot(rows, up_weight[0], preferred_element_type=jnp.float32)
    hidden = (jax.nn.silu(gate) * upper).astype(jnp.bfloat16)
    results = jnp.dot(hidden, down_weight[0], preferred_element_type=jnp.float32)
    weighted = (results.reshape(n_src, capacity, width) * slot_share[..., None]).astype(jnp.bfloat16)
    partial = jnp.einsum(
        "sqt,sqd->std", place, weighted, preferred_element_type=jnp.float32
    ).astype(jnp.bfloat16)
    return lax.psum_scatter(
        partial.reshape(n_src * n_rows, width), axes, scatter_dimension=0, tiled=True
    )


def solution(mesh):
    return jax.shard_map(
        shards,
        mesh=mesh,
        in_specs=(
            P(("rep", "grp", "loc"), None),
            P(("rep", "grp", "loc"), None),
            P(("rep", "grp", "loc"), None),
            P(("grp", "loc"), None, None),
            P(("grp", "loc"), None, None),
            P(("grp", "loc"), None, None),
        ),
        out_specs=P(("rep", "grp", "loc"), None),
        check_vma=False,
    )
```

profile of v0, /device:TPU:0, one launch (start us, length us, event | category | flops | bytes accessed | tf_op | source)
XLA Modules:
  0.0 338.3 jit_solution(7914901651433764792)
XLA Ops:
  6.5 0.0 all-gather.4.cloned.1.call-start
  6.5 0.7 all-gather.4.cloned.1.call-update
  7.3 0.0 reduce-scatter.2.cloned.1.call-start
  7.3 0.7 pad_add_fusion
  8.0 23.9 %all-gather = s32[2048,12]{0,1:T(8,128)S(1)} all-gather(s32[128,12]{0,1:T(8,128)S(1)} %pad_add_fusion), channel_id=2, replica_groups=mesh['rep'=2,'grp'=8,'loc'=2] {'grp','loc'}, dimensions={0}, use_global_device_ids=true | all-gather | bytes 104448 | tf_op jit(solution)/shard_map/all_gather | solution.py:17
  32.0 0.1 select_reduce_fusion.1
  32.1 0.3 reduce_window_sum.11
  32.4 0.4 select_reduce_fusion
  32.8 93.7 %all-gather.4.cloned.1.call-done = bf16[2048,3584]{1,0:T(8,128)(2,1)} async-done(((bf16[128,3584]{1,0:T(8,128)(2,1)}), bf16[2048,3584]{1,0:T(8,128)(2,1)}) %all-gather.4.cloned.1.call-update) | async-done | bytes 14680080 | tf_op jit(solution)/shard_map/all_gather | solution.py:18
  126.5 7.7 %convolution_convert_fusion.1 = bf16[16,80,3584]{2,1,0:T(8,128)(2,1)S(1)} fusion(bf16[16,128,3584]{2,1,0:T(8,128)(2,1)} %bitcast.30, s32[16,128]{1,0:T(8,128)S(1)} %convert_subtract_fusion, pred[16,128]{1,0:T(8,128)(4,1)S(1)} %get-tuple-element.7), kind=kOutput, calls=%fused_computation.2 | convolution fusion | flops 1179320320 | bytes 23865344 | tf_op jit(solution)/shard_map/sqt,std->sqd/dot_general | solution.py:35
  134.2 13.8 %fusion.3 = f32[1280,1024]{1,0:T(8,128)S(1)} fusion(bf16[1280,3584]{1,0:T(8,128)(2,1)S(1)} %bitcast.31, bf16[1,3584,1024]{2,1,0:T(8,128)(2,1)} %param.10), kind=kOutput, calls=%fused_computation.4 | convolution fusion | flops 9395240960 | bytes 21757952 | tf_op jit(solution)/shard_map/dot_general | solution.py:39
  148.0 14.0 %multiply_convert_fusion.1 = bf16[1280,1024]{1,0:T(8,128)(2,1)} fusion(f32[1280,1024]{1,0:T(8,128)S(1)} %fusion.3, bf16[1280,3584]{1,0:T(8,128)(2,1)S(1)} %bitcast.32, bf16[1,3584,1024]{2,1,0:T(8,128)(2,1)} %param.9), kind=kOutput, calls=%fused_computation.8 | convolution fusion | flops 9403105280 | bytes 24379392 | tf_op jit(solution)/shard_map/dot_general | solution.py:38
  162.1 21.4 %convolution_convert_fusion = bf16[16,128,3584]{2,1,0:T(8,128)(2,1)} fusion(bf16[16,80,1024]{2,1,0:T(8,128)(2,1)} %bitcast.36, f32[16,80]{1,0:T(8,128)S(1)} %select_reduce_fusion, bf16[1,1024,3584]{2,1,0:T(8,128)(2,1)} %param.11, s32[16,128]{1,0:T(8,128)S(1)} %convert_subtract_fusion, pred[16,128]{1,0:T(8,128)(4,1)S(1)} %get-tuple-element.7), kind=kOutput, calls=%fused_computation.1 | convolution fusion | flops 10586488832 | bytes 24656896 | tf_op jit(solution)/shard_map/sqt,sqd->std/dot_general | solution.py:43
  183.5 0.0 reduce-scatter.2.cloned.1.call-update
  183.5 148.0 %reduce-scatter.2.cloned.1.call-done = bf16[128,3584]{1,0:T(8,128)(2,1)} async-done(((bf16[2048,3584]{1,0:T(8,128)(2,1)}), bf16[128,3584]{1,0:T(8,128)(2,1)}) %reduce-scatter.2.cloned.1.call-update) | async-done | bytes 917520 | tf_op jit(solution)/shard_map/reduce_scatter | solution.py:46
  (8 shorter events, 0.1 us)
Async XLA Ops:
  6.5 120.0 %all-gather.4.cloned.1.call-start = ((), (), s32[]{:S(2)}) async-start(), calls=%async_computation.2 | async-start | bytes 15597568 | tf_op jit(solution)/shard_map/all_gather | solution.py:18
  7.3 324.2 %reduce-scatter.2.cloned.1.call-start = ((), (), s32[]{:S(2)}) async-start(), calls=%async_computation.1 | async-start | bytes 15597568 | tf_op jit(solution)/shard_map/reduce_scatter | solution.py:46
Sparse Core Ops, SparseCore 0:
  9.7 116.7 all-gather.3
  183.6 147.8 reduce-scatter.1
where the time goes:
time: 339 us; the launch traced here: 338 us
  waiting for transfers between devices  242 us (71%)
  matrix products  57 us (17%)
  blocking collectives  23.9 us (7%)
  between operations  13.5 us (4%)
    reduce_scatter x1, waiting for transfers between devices, shards(): lax.psum_scatter(partial.reshape(n_src * n_rows, width), axes, scatter_di...  148 us
    all_gather x1, waiting for transfers between devices, shards(): everyone = lax.all_gather(tokens, axes, axis=0, tiled=False)  93.7 us
    all_gather x1, blocking collectives, shards(): routing = lax.all_gather(routing, axes, axis=0, tiled=False)  23.9 us
    dot_general x1, matrix products, shards(): jnp.einsum('sqt,sqd->std', place, weighted, preferred_element_type=jnp.fl...  21.4 us
    dot_general x1, matrix products, shards(): gate = jnp.dot(rows, gate_weight[0], preferred_element_type=jnp.float32)  14 us
    dot_general x1, matrix products, shards(): upper = jnp.dot(rows, up_weight[0], preferred_element_type=jnp.float32)  13.8 us
    dot_general x1, matrix products, shards(): jnp.einsum('sqt,std->sqd', place, everyone, preferred_element_type=jnp.fl...  7.7 us
  transfers between devices with their start and end apart: 2, of which 2 were waited for; matrix products, arithmetic and copies ran while one was open for 0% of the time, Pallas kernels for 0%

commit v1 on v0

--- a/solution.py
+++ b/solution.py
@@ -1,7 +1,243 @@
 import jax
 import jax.numpy as jnp
 from jax import lax
+from jax.experimental import pallas as pl
+from jax.experimental.pallas import tpu as pltpu
 from jax.sharding import PartitionSpec as P
+
+MESH = pl.DeviceIdType.MESH
+LANES = 128
+
+
+def flip(bit, other):
+    return bit + other - 2 * bit * other
+
+
+def fused_kernel(
+    own, gate_hbm, up_hbm, down_hbm, out_ref,
+    tok, gate_w, up_w, down_w, hidden, keep, lsend, lrecv, yrecv, zrecv,
+    w_sem, own_sem,
+    zg_s, zg_r, yg_s, yg_r, lg_s, lg_r, lr_s, lr_r, yr_s, yr_r, zr_s, zr_r,
+):
+    n_rows, width = out_ref.shape
+    ff = hidden.shape[1]
+    steps = keep.shape[0]
+    grp = lax.axis_index("grp")
+    loc = lax.axis_index("loc")
+    y = grp % 2
+    zb = (grp // 2) % 2
+    za = grp // 4
+
+    def at_z(dz):
+        return {"grp": 4 * flip(za, dz // 2) + 2 * flip(zb, dz % 2) + y, "loc": loc}
+
+    y_peer = {"grp": grp + 1 - 2 * y, "loc": loc}
+    l_peer = {"grp": grp, "loc": 1 - loc}
+
+    def remote(src, dst, send, recv, peer):
+        return pltpu.make_async_remote_copy(
+            src_ref=src, dst_ref=dst, send_sem=send, recv_sem=recv,
+            device_id=peer, device_id_type=MESH,
+        )
+
+    def z_gather(dz):
+        return remote(own, tok.at[2 * dz, 0], zg_s.at[dz], zg_r.at[dz], at_z(dz))
+
+    def y_gather(dz, src=None):
+        src = tok.at[2 * dz, 0] if src is None else src
+        return remote(src, tok.at[2 * dz + 1, 0], yg_s.at[dz], yg_r.at[dz], y_peer)
+
+    def l_gather(s, src=None):
+        src = tok.at[s, 0] if src is None else src
+        return remote(src, tok.at[s, 1], lg_s.at[s], lg_r.at[s], l_peer)
+
+    def l_reduce(s):
+        return remote(lsend.at[s % 2], lrecv.at[s], lr_s.at[s], lr_r.at[s], l_peer)
+
+    def y_reduce(dz):
+        return remote(keep.at[2 * dz + 1], yrecv.at[dz], yr_s.at[dz], yr_r.at[dz], y_peer)
+
+    def z_reduce(dz):
+        return remote(keep.at[2 * dz], zrecv.at[dz], zr_s.at[dz], zr_r.at[dz], at_z(dz))
+
+    barrier = pltpu.get_barrier_semaphore()
+    peers = [at_z(1), at_z(2), at_z(3), y_peer, l_peer]
+    for peer in peers:
+        pl.semaphore_signal(barrier, inc=1, device_id=peer, device_id_type=MESH)
+    w_copies = [
+        pltpu.make_async_copy(gate_hbm.at[0], gate_w, w_sem.at[0]),
+        pltpu.make_async_copy(up_hbm.at[0], up_w, w_sem.at[1]),
+        pltpu.make_async_copy(down_hbm.at[0], down_w, w_sem.at[2]),
+    ]
+    own_copy = pltpu.make_async_copy(own, tok.at[0, 0], own_sem)
+    own_copy.start()
+    pl.semaphore_wait(barrier, len(peers))
+    l_gather(0, own).start()
+    y_gather(0, own).start()
+    for dz in (1, 2, 3):
+        z_gather(dz).start()
+    for copy in w_copies:
+        copy.start()
+    own_copy.wait()
+    for copy in w_copies:
+        copy.wait()
+
+    part = 16
+
+    def add_core_peer(s):
+        l_reduce(s).wait_recv()
+
+        @pl.loop(0, n_rows // part)
+        def _(r):
+            rows = pl.ds(pl.multiple_of(r * part, part), part)
+            keep[s, rows, :] = (
+                keep[s, rows, :].astype(jnp.float32) + lrecv[s, rows, :].astype(jnp.float32)
+            ).astype(jnp.bfloat16)
+
+        @pl.when(s % 2 == 1)
+        def _():
+            y_reduce(s // 2).start()
+
+    def add_y_peer(dz):
+        y_reduce(dz).wait_recv()
+
+        @pl.loop(0, n_rows // part)
+        def _(r):
+            rows = pl.ds(pl.multiple_of(r * part, part), part)
+            keep[2 * dz, rows, :] = (
+                keep[2 * dz, rows, :].astype(jnp.float32) + yrecv[dz, rows, :].astype(jnp.float32)
+            ).astype(jnp.bfloat16)
+
+        z_reduce(dz).start()
+
+    expert = 2 * grp + loc
+    tile = 256
+    span = 512
+
+    @pl.loop(0, steps)
+    def _(s):
+        dz = s // 2
+
+        @pl.when(jnp.logical_and(s % 2 == 0, s > 0))
+        def _():
+            z_gather(dz).wait_recv()
+            y_gather(dz).start()
+
+        @pl.when(s % 2 == 1)
+        def _():
+            y_gather(dz).wait_recv()
+
+        @pl.when(s > 0)
+        def _():
+            l_gather(s).start()
+            add_core_peer(s - 1)
+
+        @pl.when(s == steps - 1)
+        def _():
+            add_y_peer(1)
+
+        l_gather(s).wait_recv()
+
+        @pl.when(s > 1)
+        def _():
+            l_reduce(s - 2).wait_send()
+
+        extra = tok[s, :, :, width:].reshape(2 * n_rows, LANES).astype(jnp.float32)
+        lane = lax.broadcasted_iota(jnp.int32, (2 * n_rows, LANES), 1)
+        share = jnp.sum(jnp.where(lane == expert, extra, 0.0), axis=1, keepdims=True)
+
+        @pl.loop(0, ff // tile)
+        def _(c):
+            cols = pl.ds(pl.multiple_of(c * tile, tile), tile)
+            x = tok[s, :, :, :width].reshape(2 * n_rows, width)
+            gate = jnp.dot(x, gate_w[:, cols], preferred_element_type=jnp.float32)
+            upper = jnp.dot(x, up_w[:, cols], preferred_element_type=jnp.float32)
+            act = gate / (1.0 + jnp.exp(-gate)) * upper
+            hidden[:, cols] = act.astype(jnp.bfloat16)
+
+        @pl.loop(0, width // span)
+        def _(c):
+            cols = pl.ds(pl.multiple_of(c * span, span), span)
+            res = jnp.dot(hidden[...], down_w[:, cols], preferred_element_type=jnp.float32)
+            res = (res * share).astype(jnp.bfloat16)
+            keep[s, :, cols] = res[:n_rows]
+            lsend[s % 2, :, cols] = res[n_rows:]
+
+        l_reduce(s).start()
+
+    add_core_peer(steps - 1)
+    add_y_peer(2)
+    add_y_peer(3)
+    y_reduce(0).wait_recv()
+    for dz in (1, 2, 3):
+        z_reduce(dz).wait_recv()
+
+    @pl.loop(0, n_rows // part)
+    def _(r):
+        rows = pl.ds(pl.multiple_of(r * part, part), part)
+        total = keep[0, rows, :].astype(jnp.float32) + yrecv[0, rows, :].astype(jnp.float32)
+        for dz in (1, 2, 3):
+            total = total + zrecv[dz, rows, :].astype(jnp.float32)
+        out_ref[rows, :] = total.astype(jnp.bfloat16)
+
+    for dz in (1, 2, 3):
+        z_gather(dz).wait_send()
+        z_reduce(dz).wait_send()
+    for dz in range(4):
+        y_gather(dz, own if dz == 0 else None).wait_send()
+        y_reduce(dz).wait_send()
+    for s in range(steps):
+        l_gather(s, own if s == 0 else None).wait_send()
+    for s in (steps - 2, steps - 1):
+        l_reduce(s).wait_send()
+
+
+def fused_shards(tokens, route_groups, route_weights, gate_weight, up_weight, down_weight):
+    n_rows, width = tokens.shape
+    n_group = lax.axis_size("grp")
+    n_loc = lax.axis_size("loc")
+    top_groups = route_groups.shape[1]
+    ff = gate_weight.shape[2]
+    lane = jnp.arange(LANES, dtype=jnp.int32)
+    weights = route_weights.reshape(n_rows, top_groups, n_loc)
+    named = route_groups[:, :, None] * n_loc + jnp.arange(n_loc, dtype=jnp.int32)
+    shares = jnp.sum(
+        jnp.where(named[..., None] == lane, weights[..., None], 0), axis=(1, 2)
+    ).astype(jnp.float32) / 4096.0
+    wide = jnp.concatenate([tokens, shares.astype(jnp.bfloat16)], axis=1)
+    full = width + LANES
+    bf16 = jnp.bfloat16
+    dma = pltpu.SemaphoreType.DMA
+    return pl.pallas_call(
+        fused_kernel,
+        out_shape=jax.ShapeDtypeStruct((n_rows, width), bf16),
+        in_specs=[pl.BlockSpec(memory_space=pl.ANY)] * 4,
+        out_specs=pl.BlockSpec(memory_space=pltpu.VMEM),
+        scratch_shapes=[
+            pltpu.VMEM((n_group, 2, n_rows, full), bf16),
+            pltpu.VMEM((width, ff), bf16),
+            pltpu.VMEM((width, ff), bf16),
+            pltpu.VMEM((ff, width), bf16),
+            pltpu.VMEM((2 * n_rows, ff), bf16),
+            pltpu.VMEM((n_group, n_rows, width), bf16),
+            pltpu.VMEM((2, n_rows, width), bf16),
+            pltpu.VMEM((n_group, n_rows, width), bf16),
+            pltpu.VMEM((4, n_rows, width), bf16),
+            pltpu.VMEM((4, n_rows, width), bf16),
+            dma((3,)), dma,
+            dma((4,)), dma((4,)), dma((4,)), dma((4,)),
+            dma((8,)), dma((8,)), dma((8,)), dma((8,)),
+            dma((4,)), dma((4,)), dma((4,)), dma((4,)),
+        ],
+        compiler_params=pltpu.CompilerParams(
+            collective_id=0, has_side_effects=True, vmem_limit_bytes=65011712
+        ),
+        cost_estimate=pl.CostEstimate(
+            flops=6 * n_group * n_loc * n_rows * width * ff,
+            bytes_accessed=6 * width * ff,
+            transcendentals=n_group * n_loc * n_rows * ff,
+        ),
+    )(wide, gate_weight, up_weight, down_weight)
 
 
 def shards(tokens, route_groups, route_weights, gate_weight, up_weight, down_weight):
@@ -49,8 +285,9 @@
 
 
 def solution(mesh):
+    fits = mesh.shape["grp"] == 8 and mesh.shape["loc"] == 2
     return jax.shard_map(
-        shards,
+        fused_shards if fits else shards,
         mesh=mesh,
         in_specs=(
             P(("rep", "grp", "loc"), None),

time: 339 us -> 245 us (0.72)
  the two profiles are of different devices: /device:TPU:0 before, /device:TPU:13 now
where the time goes in v1:
time: 245 us
  Pallas kernels  239 us (98%)
  other arithmetic  3.91 us (2%)
    pallas_call x1, Pallas kernels, fused_shards(): pl.pallas_call(fused_kernel, out_shape=jax.ShapeDtypeStruct((n_rows, widt...  239 us

profile of v1, /device:TPU:13, one launch (start us, length us, event | category | flops | bytes accessed | tf_op | source)
XLA Modules:
  0.0 244.6 jit_solution(16776506077857242007)
XLA Ops:
  0.0 0.7 broadcast_multiply_fusion
  0.7 1.0 select_reduce_fusion
  1.7 2.2 pad_maximum_fusion.own
  3.9 238.5 %shard_map.64 = bf16[128,3584]{1,0:T(8,128)(2,1)} custom-call(bf16[128,3712]{1,0:T(8,128)(2,1)} %pad_maximum_fusion.own, bf16[1,3584,1024]{2,1,0:T(8,128)(2,1)} %gate_hbm.1, bf16[1,3584,1024]{2,1,0:T(8,128)(2,1)} %up_hbm.1, bf16[1,1024,3584]{2,1,0:T(8,128)(2,1)} %down_hbm.1), custom_call_target="tpu_custom_call" | custom-call | flops 45097156608 | bytes 22020096 | tf_op jit(solution)/shard_map/pallas_call | solution.py:211
  242.5 2.2 copy.10
  (2 shorter events, 0.0 us)

commit v2 on v0

--- a/solution.py
+++ b/solution.py
@@ -1,7 +1,328 @@
 import jax
 import jax.numpy as jnp
 from jax import lax
+from jax.experimental import pallas as pl
+from jax.experimental.pallas import tpu as pltpu
 from jax.sharding import PartitionSpec as P
+
+MESH = pl.DeviceIdType.MESH
+LANES = 128
+
+
+def fused_kernel(
+    own, gate_hbm, up_hbm, down_hbm, out_ref,
+    tok_a, tok_b, picked, gate_w, up_w, down_w, hidden,
+    keep_a, keep_b, lsend_a, lsend_b, lrecv_a, lrecv_b, yrecv, zrecv,
+    w_sem, own_sem, zg_s, zg_r, yg_s, yg_r, la_s, la_r, lb_s, lb_r,
+    ra_s, ra_r, rb_s, rb_r, yr_s, yr_r, zr_s, zr_r,
+):
+    n_rows, width = out_ref.shape
+    cap = picked.shape[1]
+    ff = hidden.shape[1]
+    n_z = keep_a.shape[0]
+    bf16 = jnp.bfloat16
+    grp = lax.axis_index("grp")
+    loc = lax.axis_index("loc")
+    y = grp % 2
+    z = grp // 2
+    y_grp = grp + 1 - 2 * y
+    expert = 2 * grp + loc
+    tile = 256
+    span = 512
+    part = 16
+
+    def at_z(zs):
+        return {"grp": 2 * zs + y, "loc": loc}
+
+    y_peer = {"grp": y_grp, "loc": loc}
+    l_peer = {"grp": grp, "loc": 1 - loc}
+
+    def remote(src, dst, send, recv, peer):
+        return pltpu.make_async_remote_copy(
+            src_ref=src, dst_ref=dst, send_sem=send, recv_sem=recv,
+            device_id=peer, device_id_type=MESH,
+        )
+
+    def z_gather(zs, up):
+        block = tok_a.at[zs, 0]
+        return remote(block, block, zg_s.at[zs, up], zg_r.at[zs], at_z(z + 2 * up - 1))
+
+    def z_arrival(zs):
+        block = tok_a.at[zs, 0]
+        return remote(block, block, zg_s.at[zs, 0], zg_r.at[zs], at_z(zs))
+
+    def y_gather(zs):
+        return remote(picked.at[zs], tok_b.at[zs, 0], yg_s.at[zs], yg_r.at[zs], y_peer)
+
+    def l_gather_a(zs):
+        return remote(tok_a.at[zs, 0], tok_a.at[zs, 1], la_s.at[zs], la_r.at[zs], l_peer)
+
+    def l_gather_b(zs):
+        return remote(tok_b.at[zs, 0], tok_b.at[zs, 1], lb_s.at[zs], lb_r.at[zs], l_peer)
+
+    def l_reduce_a(zs):
+        return remote(lsend_a, lrecv_a.at[zs], ra_s.at[zs], ra_r.at[zs], l_peer)
+
+    def l_reduce_b(zs):
+        return remote(lsend_b, lrecv_b.at[zs], rb_s.at[zs], rb_r.at[zs], l_peer)
+
+    def y_reduce(zs):
+        return remote(keep_b.at[zs], yrecv.at[zs], yr_s.at[zs], yr_r.at[zs], y_peer)
+
+    def z_reduce(zs, slot):
+        return remote(keep_a.at[zs], zrecv.at[slot], zr_s.at[zs], zr_r.at[slot], at_z(zs))
+
+    def order(k):
+        m = (z % 2) * (1 - z // 2) + (1 - z % 2) * (z // 2)
+        v = k + m * (1 - k // 2) * (1 - 2 * k)
+        return v + (z // 2) * (3 - 2 * v)
+
+    def column(extra, lane_index):
+        lane = lax.broadcasted_iota(jnp.int32, extra.shape, 1)
+        return jnp.sum(
+            jnp.where(lane == lane_index, extra.astype(jnp.float32), 0.0), axis=1, keepdims=True
+        )
+
+    def placer(zs, lanes):
+        slot = column(tok_a[zs, 0, :, width:], LANES // 2 + y_grp)
+        lane = lax.broadcasted_iota(jnp.int32, (n_rows, lanes), 1).astype(jnp.float32)
+        return jnp.where(slot == lane + 1.0, 1.0, 0.0)
+
+    def pick(zs):
+        place = placer(zs, n_rows).T.astype(bf16)[:cap]
+
+        def some(cols):
+            picked[zs, :, cols] = jnp.dot(
+                place, tok_a[zs, 0, :, cols], preferred_element_type=jnp.float32
+            ).astype(bf16)
+
+        @pl.loop(0, width // span)
+        def _(c):
+            some(pl.ds(pl.multiple_of(c * span, span), span))
+
+        some(pl.ds(width, LANES))
+
+    def run_expert(tok, zs, keep, lsend):
+        rows = tok.shape[2]
+        share = column(tok[zs, :, :, width:].reshape(2 * rows, LANES), expert)
+
+        @pl.loop(0, ff // tile)
+        def _(c):
+            cols = pl.ds(pl.multiple_of(c * tile, tile), tile)
+            x = tok[zs, :, :, :width].reshape(2 * rows, width)
+            gate = jnp.dot(x, gate_w[:, cols], preferred_element_type=jnp.float32)
+            upper = jnp.dot(x, up_w[:, cols], preferred_element_type=jnp.float32)
+            act = gate / (1.0 + jnp.exp(-gate)) * upper
+            hidden[: 2 * rows, cols] = act.astype(bf16)
+
+        @pl.loop(0, width // span)
+        def _(c):
+            cols = pl.ds(pl.multiple_of(c * span, span), span)
+            res = jnp.dot(
+                hidden[: 2 * rows, :], down_w[:, cols], preferred_element_type=jnp.float32
+            )
+            res = (res * share).astype(bf16)
+            keep[zs, :, cols] = res[:rows]
+            lsend[:, cols] = res[rows:]
+
+    def add_core_peer(keep, lrecv, zs):
+        @pl.loop(0, keep.shape[1] // part)
+        def _(r):
+            rows = pl.ds(pl.multiple_of(r * part, part), part)
+            keep[zs, rows, :] = (
+                keep[zs, rows, :].astype(jnp.float32) + lrecv[zs, rows, :].astype(jnp.float32)
+            ).astype(bf16)
+
+    def add_y_peer(zs):
+        y_reduce(zs).wait_recv()
+        place = placer(zs, cap).astype(bf16)
+
+        @pl.loop(0, width // span)
+        def _(c):
+            cols = pl.ds(pl.multiple_of(c * span, span), span)
+            spread = jnp.dot(place, yrecv[zs, :, cols], preferred_element_type=jnp.float32)
+            keep_a[zs, :, cols] = (keep_a[zs, :, cols].astype(jnp.float32) + spread).astype(bf16)
+
+    barrier = pltpu.get_barrier_semaphore()
+    peers = [at_z((z + j) % n_z) for j in range(1, n_z)] + [y_peer, l_peer]
+    own_copy = pltpu.make_async_copy(own, tok_a.at[z, 0], own_sem)
+    own_copy.start()
+    for peer in peers:
+        pl.semaphore_signal(barrier, inc=1, device_id=peer, device_id_type=MESH)
+    w_copies = [
+        pltpu.make_async_copy(gate_hbm.at[0], gate_w, w_sem.at[0]),
+        pltpu.make_async_copy(up_hbm.at[0], up_w, w_sem.at[1]),
+        pltpu.make_async_copy(down_hbm.at[0], down_w, w_sem.at[2]),
+    ]
+    own_copy.wait()
+    for copy in w_copies:
+        copy.start()
+    pl.semaphore_wait(barrier, len(peers))
+
+    @pl.loop(0, n_z + 1)
+    def _(k):
+        zs = order(k)
+        zp = order(k - 1)
+
+        @pl.when(k < n_z)
+        def _():
+            @pl.when(k > 0)
+            def _():
+                z_arrival(zs).wait_recv()
+
+            @pl.when(jnp.logical_and(zs <= z, z < n_z - 1))
+            def _():
+                z_gather(zs, 1).start()
+
+            @pl.when(jnp.logical_and(zs >= z, z > 0))
+            def _():
+                z_gather(zs, 0).start()
+
+            l_gather_a(zs).start()
+            pick(zs)
+            y_gather(zs).start()
+
+        @pl.when(k == 0)
+        def _():
+            for copy in w_copies:
+                copy.wait()
+
+        @pl.when(k > 0)
+        def _():
+            y_gather(zp).wait_recv()
+            l_gather_b(zp).start()
+
+        @pl.when(k < n_z)
+        def _():
+            l_gather_a(zs).wait_recv()
+
+            @pl.when(k > 0)
+            def _():
+                l_reduce_a(zp).wait_send()
+
+            run_expert(tok_a, zs, keep_a, lsend_a)
+            l_reduce_a(zs).start()
+
+        @pl.when(k > 0)
+        def _():
+            l_gather_b(zp).wait_recv()
+
+            @pl.when(k > 1)
+            def _():
+                l_reduce_b(order(k - 2)).wait_send()
+
+            run_expert(tok_b, zp, keep_b, lsend_b)
+            l_reduce_b(zp).start()
+
+        @pl.when(k < n_z)
+        def _():
+            l_reduce_a(zs).wait_recv()
+            add_core_peer(keep_a, lrecv_a, zs)
+
+        @pl.when(k > 0)
+        def _():
+            l_reduce_b(zp).wait_recv()
+            add_core_peer(keep_b, lrecv_b, zp)
+            y_reduce(zp).start()
+
+        @pl.when(k > 1)
+        def _():
+            add_y_peer(order(k - 2))
+
+        @pl.when(k > 2)
+        def _():
+            z_reduce(order(k - 2), z).start()
+
+    last = order(n_z - 1)
+    add_y_peer(last)
+    z_reduce(last, z).start()
+    others = [(z + j) % n_z for j in range(1, n_z)]
+    for zs in others:
+        z_reduce(zs, zs).wait_recv()
+
+    @pl.loop(0, n_rows // part)
+    def _(r):
+        rows = pl.ds(pl.multiple_of(r * part, part), part)
+        total = keep_a[z, rows, :].astype(jnp.float32)
+        for zs in others:
+            total = total + zrecv[zs, rows, :].astype(jnp.float32)
+        out_ref[rows, :] = total.astype(bf16)
+
+    for zs in others:
+        z_reduce(zs, z).wait_send()
+    l_reduce_a(last).wait_send()
+    l_reduce_b(last).wait_send()
+
+    @pl.loop(0, n_z)
+    def _(zs):
+        @pl.when(jnp.logical_and(zs <= z, z < n_z - 1))
+        def _():
+            z_gather(zs, 1).wait_send()
+
+        @pl.when(jnp.logical_and(zs >= z, z > 0))
+        def _():
+            z_gather(zs, 0).wait_send()
+
+        y_gather(zs).wait_send()
+        y_reduce(zs).wait_send()
+        l_gather_a(zs).wait_send()
+        l_gather_b(zs).wait_send()
+
+
+def fused_shards(tokens, route_groups, route_weights, gate_weight, up_weight, down_weight):
+    n_rows, width = tokens.shape
+    n_group = lax.axis_size("grp")
+    n_loc = lax.axis_size("loc")
+    top_groups = route_groups.shape[1]
+    cap = n_rows * top_groups * 5 // (n_group * 4)
+    ff = gate_weight.shape[2]
+    half = LANES // 2
+    lane = jnp.arange(half, dtype=jnp.int32)
+    weights = route_weights.reshape(n_rows, top_groups, n_loc)
+    named = route_groups[:, :, None] * n_loc + jnp.arange(n_loc, dtype=jnp.int32)
+    shares = jnp.sum(
+        jnp.where(named[..., None] == lane, weights[..., None], 0), axis=(1, 2)
+    ).astype(jnp.float32) / 4096.0
+    chosen = jnp.any(route_groups[:, :, None] == lane, axis=1)
+    slots = jnp.where(chosen, jnp.cumsum(chosen.astype(jnp.int32), axis=0), 0)
+    bf16 = jnp.bfloat16
+    wide = jnp.concatenate([tokens, shares.astype(bf16), slots.astype(bf16)], axis=1)
+    full = width + LANES
+    n_z = n_group // 2
+    vmem = pltpu.VMEM
+    dma = pltpu.SemaphoreType.DMA
+    return pl.pallas_call(
+        fused_kernel,
+        out_shape=jax.ShapeDtypeStruct((n_rows, width), bf16),
+        in_specs=[pl.BlockSpec(memory_space=pl.ANY)] * 4,
+        out_specs=pl.BlockSpec(memory_space=pltpu.VMEM),
+        scratch_shapes=[
+            vmem((n_z, 2, n_rows, full), bf16),
+            vmem((n_z, 2, cap, full), bf16),
+            vmem((n_z, cap, full), bf16),
+            vmem((width, ff), bf16),
+            vmem((width, ff), bf16),
+            vmem((ff, width), bf16),
+            vmem((2 * n_rows, ff), bf16),
+            vmem((n_z, n_rows, width), bf16),
+            vmem((n_z, cap, width), bf16),
+            vmem((n_rows, width), bf16),
+            vmem((cap, width), bf16),
+            vmem((n_z, n_rows, width), bf16),
+            vmem((n_z, cap, width), bf16),
+            vmem((n_z, cap, width), bf16),
+            vmem((n_z, n_rows, width), bf16),
+            dma((3,)), dma, dma((n_z, 2)), dma((n_z,)),
+        ] + [dma((n_z,))] * 14,
+        compiler_params=pltpu.CompilerParams(
+            collective_id=0, has_side_effects=True, vmem_limit_bytes=65011712
+        ),
+        cost_estimate=pl.CostEstimate(
+            flops=6 * n_group * (n_rows + cap) * width * ff,
+            bytes_accessed=6 * width * ff,
+            transcendentals=n_group * (n_rows + cap) * ff,
+        ),
+    )(wide, gate_weight, up_weight, down_weight)
 
 
 def shards(tokens, route_groups, route_weights, gate_weight, up_weight, down_weight):
@@ -49,8 +370,9 @@
 
 
 def solution(mesh):
+    fits = mesh.shape["grp"] == 8 and mesh.shape["loc"] == 2
     return jax.shard_map(
-        shards,
+        fused_shards if fits else shards,
         mesh=mesh,
         in_specs=(
             P(("rep", "grp", "loc"), None),

time: 339 us -> 199 us (0.59)
  waiting for transfers between devices: 242 us -> 0 us
  Pallas kernels: 0 us -> 192 us
  matrix products: 57 us -> 0 us
  blocking collectives: 23.9 us -> 0 us
  between operations: 13.5 us -> 0.06 us
  local copies, waits for them, and re-layouts: 0.03 us -> 4.5 us
    pallas_call x0 -> x1, Pallas kernels: none -> 192 us  [fused_shards(): pl.pallas_call(fused_kernel, out_shape=jax.ShapeDtypeStruct((n_rows, widt...]
    reduce_scatter x1 -> x0, waiting for transfers between devices: 148 us -> none  [shards(): lax.psum_scatter(partial.reshape(n_src * n_rows, width), axes, scatter_di...]
    all_gather x1 -> x0, waiting for transfers between devices: 93.7 us -> none  [shards(): everyone = lax.all_gather(tokens, axes, axis=0, tiled=False)]
    dot_general x4 -> x0, matrix products: 57 us -> none  [the longest x1 21.4 us: shards(): jnp.einsum('sqt,sqd->std', place, weighted, preferred_element_type=jnp.fl...]
    all_gather x1 -> x0, blocking collectives: 23.9 us -> none  [shards(): routing = lax.all_gather(routing, axes, axis=0, tiled=False)]
  transfers between devices with their start and end apart: 2 -> 0, of which waited for: 2 -> 0; matrix products, arithmetic and copies ran while one was open for 0% -> 0% of each run, Pallas kernels for 0% -> 0%
where the time goes in v2:
time: 199 us; the launch traced here: 198 us
  Pallas kernels  192 us (96%)
  local copies, waits for them, and re-layouts  4.5 us (2%)
  other arithmetic  2.32 us (1%)
    pallas_call x1, Pallas kernels, fused_shards(): pl.pallas_call(fused_kernel, out_shape=jax.ShapeDtypeStruct((n_rows, widt...  192 us

profile of v2, /device:TPU:0, one launch (start us, length us, event | category | flops | bytes accessed | tf_op | source)
XLA Modules:
  0.0 198.5 jit_solution(11620011862056459074)
XLA Ops:
  0.0 0.7 broadcast_multiply_fusion
  0.7 0.7 fusion
  1.4 0.1 copy.15
  1.5 0.7 select_reduce_fusion
  2.3 0.1 copy.13
  2.4 0.1 copy.14
  2.5 0.2 reduce_window_sum.11
  2.7 2.0 %concatenate.3.own = bf16[128,3712]{1,0:T(8,128)(2,1)} concatenate(bf16[128,3584]{1,0:T(8,128)(2,1)} %param.6, bf16[128,64]{1,0:T(8,128)(2,1)S(1)} %multiply_convert_fusion, bf16[128,64]{1,0:T(8,128)(2,1)S(1)} %select_convert_fusion), dimensions={1} | concatenate | bytes 1900544 | tf_op jit(solution)/shard_map/concatenate | solution.py:289
  4.7 191.6 %shard_map.64 = bf16[128,3584]{1,0:T(8,128)(2,1)} custom-call(bf16[128,3712]{1,0:T(8,128)(2,1)} %concatenate.3.own, bf16[1,3584,1024]{2,1,0:T(8,128)(2,1)} %gate_hbm.1, bf16[1,3584,1024]{2,1,0:T(8,128)(2,1)} %up_hbm.1, bf16[1,1024,3584]{2,1,0:T(8,128)(2,1)} %down_hbm.1), custom_call_target="tpu_custom_call" | custom-call | flops 36641439744 | bytes 22020096 | tf_op jit(solution)/shard_map/pallas_call | solution.py:294
  196.3 2.2 %copy.17 = bf16[128,3584]{1,0:T(8,128)(2,1)} copy(bf16[128,3584]{1,0:T(8,128)(2,1)} %shard_map.64) | data formatting | bytes 1835008
  (5 shorter events, 0.0 us)

commit v3 on v2

--- a/solution.py
+++ b/solution.py
@@ -26,6 +26,7 @@
     y = grp % 2
     z = grp // 2
     y_grp = grp + 1 - 2 * y
+    inner = (z % 2) * (1 - z // 2) + (1 - z % 2) * (z // 2)
     expert = 2 * grp + loc
     tile = 256
     span = 512
@@ -73,8 +74,7 @@
         return remote(keep_a.at[zs], zrecv.at[slot], zr_s.at[zs], zr_r.at[slot], at_z(zs))
 
     def order(k):
-        m = (z % 2) * (1 - z // 2) + (1 - z % 2) * (z // 2)
-        v = k + m * (1 - k // 2) * (1 - 2 * k)
+        v = k + inner * (1 - k // 3) * (1 - 3 * (k // 2))
         return v + (z // 2) * (3 - 2 * v)
 
     def column(extra, lane_index):
@@ -159,6 +159,19 @@
         copy.start()
     pl.semaphore_wait(barrier, len(peers))
 
+    def pass_on(zs, arrives):
+        @pl.when(arrives)
+        def _():
+            z_arrival(zs).wait_recv()
+
+        @pl.when(jnp.logical_and(zs <= z, z < n_z - 1))
+        def _():
+            z_gather(zs, 1).start()
+
+        @pl.when(jnp.logical_and(zs >= z, z > 0))
+        def _():
+            z_gather(zs, 0).start()
+
     @pl.loop(0, n_z + 1)
     def _(k):
         zs = order(k)
@@ -166,17 +179,13 @@
 
         @pl.when(k < n_z)
         def _():
-            @pl.when(k > 0)
+            @pl.when(jnp.logical_or(k != 2, inner == 0))
             def _():
-                z_arrival(zs).wait_recv()
-
-            @pl.when(jnp.logical_and(zs <= z, z < n_z - 1))
+                pass_on(zs, k > 0)
+
+            @pl.when(jnp.logical_and(k == 1, inner == 1))
             def _():
-                z_gather(zs, 1).start()
-
-            @pl.when(jnp.logical_and(zs >= z, z > 0))
-            def _():
-                z_gather(zs, 0).start()
+                pass_on(order(2), True)
 
             l_gather_a(zs).start()
             pick(zs)

time: 199 us -> 191 us (0.960)
  Pallas kernels: 192 us -> 184 us
    pallas_call x1, Pallas kernels: 192 us -> 184 us  [fused_shards(): pl.pallas_call(fused_kernel, out_shape=jax.ShapeDtypeStruct((n_rows, widt...]
where the time goes in v3:
time: 191 us
  Pallas kernels  184 us (96%)
  local copies, waits for them, and re-layouts  4.5 us (2%)
  other arithmetic  2.32 us (1%)
    pallas_call x1, Pallas kernels, fused_shards(): pl.pallas_call(fused_kernel, out_shape=jax.ShapeDtypeStruct((n_rows, widt...  184 us

profile of v3, /device:TPU:0, one launch (start us, length us, event | category | flops | bytes accessed | tf_op | source)
XLA Modules:
  0.0 191.1 jit_solution(16114724409877951195)
XLA Ops:
  0.0 0.7 broadcast_multiply_fusion
  0.7 0.7 fusion
  1.4 0.1 copy.15
  1.5 0.7 select_reduce_fusion
  2.3 0.1 copy.13
  2.4 0.1 copy.14
  2.5 0.2 reduce_window_sum.11
  2.7 2.0 %concatenate.3.own = bf16[128,3712]{1,0:T(8,128)(2,1)} concatenate(bf16[128,3584]{1,0:T(8,128)(2,1)} %param.6, bf16[128,64]{1,0:T(8,128)(2,1)S(1)} %multiply_convert_fusion, bf16[128,64]{1,0:T(8,128)(2,1)S(1)} %select_convert_fusion), dimensions={1} | concatenate | bytes 1900544 | tf_op jit(solution)/shard_map/concatenate | solution.py:298
  4.7 184.2 %shard_map.64 = bf16[128,3584]{1,0:T(8,128)(2,1)} custom-call(bf16[128,3712]{1,0:T(8,128)(2,1)} %concatenate.3.own, bf16[1,3584,1024]{2,1,0:T(8,128)(2,1)} %gate_hbm.1, bf16[1,3584,1024]{2,1,0:T(8,128)(2,1)} %up_hbm.1, bf16[1,1024,3584]{2,1,0:T(8,128)(2,1)} %down_hbm.1), custom_call_target="tpu_custom_call" | custom-call | flops 36641439744 | bytes 22020096 | tf_op jit(solution)/shard_map/pallas_call | solution.py:303
  189.0 2.2 %copy.17 = bf16[128,3584]{1,0:T(8,128)(2,1)} copy(bf16[128,3584]{1,0:T(8,128)(2,1)} %shard_map.64) | data formatting | bytes 1835008
  (5 shorter events, 0.0 us)
